TPU v7x, 32 devices: a whole 2x2x4 slice. The times are simulated.
32 devices in a mesh: gx: 4 (over x, core), yz: 8 (over z, y).
Axes of the slice: x: 2, y: 2, z: 4, core: 2. Of those that a mesh axis runs over, the one named last changes fastest.
Arguments:
- right_side: float32 [3, 32, 1024, 256], P(None, 'gx', 'yz'), may hold values from -30 to 30
- viscosity: bfloat16 [32, 1024, 256], P('gx', 'yz'), may hold values from 0.29882812 to 3
- strain_rate: bfloat16 [6, 32, 1024, 256], P(None, 'gx', 'yz'), may hold values from -6 to 6
- cell_code: int32 [32, 1024, 256], P('gx', 'yz'), may hold values from 0 to 2
Outputs:
- solution_field: float32 [3, 32, 1024, 256], P(None, 'gx', 'yz')
- residual: float32 [3, 32, 1024, 256], P(None, 'gx', 'yz')
All inputs are finite; a program needn't handle non-finite values.
Results may differ from a plain program's by a relative error of at most 0.0003.
Values may be sent and summed in bfloat16 or wider, within the bound.
A program may use at most 128 MiB of HBM per device.

v0:
```python
import jax
import jax.numpy as jnp
from jax import lax
from jax.sharding import PartitionSpec as P

ITERS = 3


SOFTEN = 0.8


def from_behind(x, axis, by):
    peers = lax.axis_size(axis)
    pairs = [(i, i + by) for i in range(peers) if 0 <= i + by < peers]
    return lax.ppermute(x, axis, pairs)


def stresses(base, next_x, next_y, next_z, viscosity, strain_rate):
    along_x = next_x - base
    along_y = next_y - base
    along_z = next_z - base
    strain = strain_rate.astype(jnp.float32)
    two_eta = 2.0 * viscosity.astype(jnp.float32)
    parts = [
        along_x[0],
        along_y[1],
        along_z[2],
        0.5 * (along_y[0] + along_x[1]),
        0.5 * (along_z[0] + along_x[2]),
        0.5 * (along_z[1] + along_y[2]),
    ]
    self_dot = (
        strain[0] * strain[0]
        + strain[1] * strain[1]
        + strain[2] * strain[2]
        + 2.0 * (strain[3] * strain[3] + strain[4] * strain[4] + strain[5] * strain[5])
    )
    cross_dot = (
        strain[0] * parts[0]
        + strain[1] * parts[1]
        + strain[2] * parts[2]
        + 2.0 * (strain[3] * parts[3] + strain[4] * parts[4] + strain[5] * parts[5])
    )
    factor = SOFTEN * cross_dot / (1.0 + self_dot)
    taus = [two_eta * (parts[k] - factor * strain[k]) for k in range(6)]
    flux_x = jnp.stack([taus[0], taus[3], taus[4]])
    flux_y = jnp.stack([taus[3], taus[1], taus[5]])
    flux_z = jnp.stack([taus[4], taus[5], taus[2]])
    return (flux_x, flux_y, flux_z)


def divergence(own_x, prev_x, own_y, prev_y, own_z, prev_z):
    return prev_x - own_x + (prev_y - own_y) + (prev_z - own_z)


def operate_shifts(field, viscosity, strain_rate, mask, weight):
    masked = mask * field
    zero_z = jnp.zeros_like(masked[..., :1])
    face_x = from_behind(masked[:, :1], "gx", -1)
    face_y = from_behind(masked[:, :, :1], "yz", -1)
    next_x = jnp.concatenate([masked[:, 1:], face_x], 1)
    next_y = jnp.concatenate([masked[:, :, 1:], face_y], 2)
    next_z = jnp.concatenate([masked[..., 1:], zero_z], 3)
    flux_x, flux_y, flux_z = stresses(masked, next_x, next_y, next_z, viscosity, strain_rate)
    lower_x = from_behind(flux_x[:, -1:], "gx", 1)
    lower_y = from_behind(flux_y[:, :, -1:], "yz", 1)
    prev_x = jnp.concatenate([lower_x, flux_x[:, :-1]], 1)
    prev_y = jnp.concatenate([lower_y, flux_y[:, :, :-1]], 2)
    prev_z = jnp.concatenate([zero_z, flux_z[..., :-1]], 3)
    return mask * divergence(flux_x, prev_x, flux_y, prev_y, flux_z, prev_z) + weight * field


def per_device(right_side, viscosity, strain_rate, cell_code):
    mask = (cell_code != 0).astype(jnp.float32)
    weight = jnp.where(cell_code == 0, 1.0, jnp.where(cell_code == 1, 0.2, 1.2)).astype(jnp.float32)
    solution_field = jnp.zeros_like(right_side)
    residual = right_side

    def squares(vector):
        return lax.psum(jnp.sum(vector * vector), ("gx", "yz"))

    direction = right_side
    norm_now = squares(residual)
    for iteration in range(ITERS):
        image = operate_shifts(direction, viscosity, strain_rate, mask, weight)
        alpha = norm_now / lax.psum(jnp.sum(direction * image), ("gx", "yz"))
        solution_field = solution_field + alpha * direction
        residual = residual - alpha * image
        norm_next = squares(residual)
        direction = residual + norm_next / norm_now * direction
        norm_now = norm_next
    return (solution_field, residual)


def solution(mesh):
    placed = (
        P(None, "gx", "yz", None),
        P("gx", "yz", None),
        P(None, "gx", "yz", None),
        P("gx", "yz", None),
    )
    return jax.shard_map(
        per_device,
        mesh=mesh,
        in_specs=placed,
        out_specs=(P(None, "gx", "yz", None), P(None, "gx", "yz", None)),
        check_vma=False,
    )
```

profile of v0, /device:TPU:0, one launch (start us, length us, event | category | flops | bytes accessed | tf_op | source)
XLA Modules:
  0.0 331.2 jit_solution(4460183115878327991)
XLA Ops:
  0.6 1.3 compare_convert_fusion
  2.0 2.6 broadcast_multiply_fusion.2
  4.6 0.0 copy-start.5
  4.6 1.3 collective-permute-start
  6.0 1.3 collective-permute-start.1
  7.3 0.3 slice.323
  7.6 0.0 copy-start.15
  7.6 0.9 slice.327
  8.5 1.0 copy-done.15
  9.5 0.8 convert_element_type.15
  10.3 0.0 copy-start.8
  10.3 2.3 collective-permute-done.1
  12.6 1.8 slice-done.4
  14.5 2.1 maximum_subtract_fusion
  16.5 1.8 multiply_bitcast_fusion.12
  18.3 1.5 multiply_bitcast_fusion.17
  19.8 0.0 copy-start.14
  19.9 1.2 pad_maximum_fusion
  21.1 3.1 collective-permute-start.2
  24.2 5.5 %collective-permute-start.3 = (f32[3,8,1,256]{3,2,1,0:T(1,128)S(1)}, f32[3,8,1,256]{3,2,1,0:T(1,128)S(1)}, u32[]{:S(2)}, u32[]{:S(2)}) collective-permute-start(f32[3,8,1,256]{3,2,1,0:T(1,128)S(1)} %slice.340), channel_id=1, source_target_pairs={{0,1},{1,2},{2,3},{3,4},{4,5},{5,6},{6,7},{8,9},{9,10},{10,11},{11... | collective-permute-start | bytes 73736 | tf_op jit(solution)/shard_map/ppermute | solution.py:15
  29.7 0.2 select_select_fusion
  29.9 0.2 slice.339
  30.1 1.1 collective-permute-done.3
  31.2 4.4 %multiply_reduce_fusion.4 = (f32[]{:T(128)}, f32[]{:T(128)}, f32[3,8,128,256]{3,2,1,0:T(8,128)}) fusion(f32[3,8,128,256]{3,2,1,0:T(8,128)S(1)} %copy-done.1, f32[8,128,256]{2,1,0:T(8,128)S(1)} %select_select_fusion, f32[1,8,128,256]{3,2,1,0:T(8,128)S(1)} %get-tuple-element.21, f32[1,8,128,256]{3,2,1,0:T(8,128)S(1)} %get-tuple-element.35, ...), kind=kLoop, calls=%fused_computation.45 | loop fusion | flops 15728638 | bytes 24104968 | tf_op jit(solution)/shard_map/reduce_sum | solution.py:86
  35.6 43.0 %all-reduce.6 = (f32[]{:T(128)}, f32[]{:T(128)}) all-reduce(f32[]{:T(128)} %get-tuple-element.3, f32[]{:T(128)} %get-tuple-element.2), channel_id=1, replica_groups=mesh['gx'=4,'yz'=8] {'gx','yz'}, use_global_device_ids=true, to_apply=%region_1.2 | all-reduce | flops 2 | bytes 16 | tf_op jit(solution)/shard_map/psum | solution.py:80
  80.0 3.3 multiply_reduce_fusion.3
  83.3 41.5 %psum.44 = f32[]{:T(128)} all-reduce(f32[]{:T(128)} %multiply_reduce_fusion.3), channel_id=1, replica_groups=mesh['gx'=4,'yz'=8] {'gx','yz'}, use_global_device_ids=true, to_apply=%region_5.6 | all-reduce | flops 1 | bytes 8 | tf_op jit(solution)/shard_map/psum | solution.py:80
  126.1 2.9 broadcast_multiply_fusion.1
  129.0 1.3 collective-permute-start.4
  130.3 1.5 collective-permute-start.5
  131.8 1.7 slice.343
  133.5 0.9 slice.349
  134.4 0.3 slice.346
  134.7 1.8 collective-permute-done.5
  136.6 3.1 maximum_subtract_fusion.4
  139.7 1.6 multiply_bitcast_fusion.6
  141.3 1.2 multiply_bitcast_fusion.11
  142.6 1.2 pad_maximum_fusion.3
  143.8 4.3 %collective-permute-start.6 = (f32[3,1,128,256]{3,2,1,0:T(8,128)S(1)}, f32[3,1,128,256]{3,2,1,0:T(8,128)S(1)}, u32[]{:S(2)}, u32[]{:S(2)}) collective-permute-start(f32[3,1,128,256]{3,2,1,0:T(8,128)S(1)} %slice.357), channel_id=1, source_target_pairs={{0,8},{8,16},{16,24},{1,9},{9,17},{17,25},{2,10},{10,18},{18,26},{... | collective-permute-start | bytes 1179656 | tf_op jit(solution)/shard_map/ppermute | solution.py:15
  148.1 3.3 collective-permute-start.7
  151.5 0.2 slice.358
  151.7 1.3 collective-permute-done.7
  153.0 4.5 %multiply_reduce_fusion.2 = (f32[]{:T(128)}, f32[3,8,128,256]{3,2,1,0:T(8,128)}) fusion(f32[3,8,128,256]{3,2,1,0:T(8,128)S(1)} %get-tuple-element.19, f32[8,128,256]{2,1,0:T(8,128)S(1)} %copy-done.12, f32[1,8,128,256]{3,2,1,0:T(8,128)S(1)} %get-tuple-element.16, f32[1,8,128,256]{3,2,1,0:T(8,128)S(1)} %get-tuple-element.30, ...), kind=kLoop, calls=%fused_computation.40 | loop fusion | flops 14155775 | bytes 24104964 | tf_op jit(solution)/shard_map/reduce_sum | solution.py:86
  157.5 41.5 %psum.45 = f32[]{:T(128)} all-reduce(f32[]{:T(128)} %get-tuple-element.14), channel_id=1, replica_groups=mesh['gx'=4,'yz'=8] {'gx','yz'}, use_global_device_ids=true, to_apply=%region_7.8 | all-reduce | flops 1 | bytes 8 | tf_op jit(solution)/shard_map/psum | solution.py:86
  200.2 6.1 %multiply_reduce_fusion.1 = (f32[]{:T(128)}, f32[3,8,128,256]{3,2,1,0:T(8,128)}) fusion(f32[3,8,128,256]{3,2,1,0:T(8,128)} %get-tuple-element.15, f32[]{:T(128)S(6)} %div.28, f32[3,8,128,256]{3,2,1,0:T(8,128)S(1)} %copy-done.1, f32[3,8,128,256]{3,2,1,0:T(8,128)} %get-tuple-element.20, f32[]{:T(128)S(6)} %div.25), kind=kLoop, calls=%fused_computation.38 | loop fusion | flops 4718591 | bytes 12582924 | tf_op jit(solution)/shard_map/reduce_sum | solution.py:80
  206.3 39.8 %psum.46 = f32[]{:T(128)} all-reduce(f32[]{:T(128)} %get-tuple-element.12), channel_id=1, replica_groups=mesh['gx'=4,'yz'=8] {'gx','yz'}, use_global_device_ids=true, to_apply=%region_9.10 | all-reduce | flops 1 | bytes 8 | tf_op jit(solution)/shard_map/psum | solution.py:80
  247.3 3.8 %broadcast_multiply_fusion = (f32[3,8,128,256]{3,2,1,0:T(8,128)S(1)}, f32[3,8,128,256]{3,2,1,0:T(8,128)S(1)}) fusion(f32[8,128,256]{2,1,0:T(8,128)} %copy-done.2, f32[3,8,128,256]{3,2,1,0:T(8,128)} %get-tuple-element.13, f32[3,8,128,256]{3,2,1,0:T(8,128)} %copy-done.6, f32[]{:T(128)S(6)} %div.29), kind=kLoop, calls=%fused_computation.48 | loop fusion | flops 2359296 | bytes 13631492 | tf_op jit(solution)/shard_map/mul | solution.py:57
  251.1 1.3 collective-permute-start.8
  252.4 1.5 collective-permute-start.9
  253.9 0.3 slice.362
  254.2 0.9 slice.368
  255.1 0.3 slice.365
  255.4 3.2 collective-permute-done.9
  258.6 2.2 maximum_subtract_fusion.8
  260.8 1.8 multiply_bitcast_fusion
  262.6 1.5 multiply_bitcast_fusion.5
  264.1 0.9 pad_maximum_fusion.6
  265.1 4.3 %collective-permute-start.10 = (f32[3,1,128,256]{3,2,1,0:T(8,128)S(1)}, f32[3,1,128,256]{3,2,1,0:T(8,128)S(1)}, u32[]{:S(2)}, u32[]{:S(2)}) collective-permute-start(f32[3,1,128,256]{3,2,1,0:T(8,128)S(1)} %slice.376), channel_id=1, source_target_pairs={{0,8},{8,16},{16,24},{1,9},{9,17},{17,25},{2,10},{10,18},{18,26},{... | collective-permute-start | bytes 1179656 | tf_op jit(solution)/shard_map/ppermute | solution.py:15
  269.4 3.9 %collective-permute-start.11 = (f32[3,8,1,256]{3,2,1,0:T(1,128)S(1)}, f32[3,8,1,256]{3,2,1,0:T(1,128)S(1)}, u32[]{:S(2)}, u32[]{:S(2)}) collective-permute-start(f32[3,8,1,256]{3,2,1,0:T(1,128)S(1)} %slice.378), channel_id=1, source_target_pairs={{0,1},{1,2},{2,3},{3,4},{4,5},{5,6},{6,7},{8,9},{9,10},{10,11},{11... | collective-permute-start | bytes 73736 | tf_op jit(solution)/shard_map/ppermute | solution.py:15
  273.3 0.2 slice.377
  273.5 1.3 collective-permute-done.11
  274.8 4.2 %multiply_reduce_fusion = (f32[]{:T(128)}, f32[3,8,128,256]{3,2,1,0:T(8,128)}) fusion(f32[3,8,128,256]{3,2,1,0:T(8,128)S(1)} %get-tuple-element.11, f32[8,128,256]{2,1,0:T(8,128)S(1)} %copy-done.13, f32[1,8,128,256]{3,2,1,0:T(8,128)S(1)} %get-tuple-element.8, f32[1,8,128,256]{3,2,1,0:T(8,128)S(1)} %get-tuple-element.25, ...), kind=kLoop, calls=%fused_computation.35 | loop fusion | flops 14155775 | bytes 24104964 | tf_op jit(solution)/shard_map/reduce_sum | solution.py:86
  279.0 41.6 %psum.47 = f32[]{:T(128)} all-reduce(f32[]{:T(128)} %get-tuple-element.6), channel_id=1, replica_groups=mesh['gx'=4,'yz'=8] {'gx','yz'}, use_global_device_ids=true, to_apply=%region_11.12 | all-reduce | flops 1 | bytes 8 | tf_op jit(solution)/shard_map/psum | solution.py:86
  321.7 9.5 %multiply_subtract_fusion = (f32[3,8,128,256]{3,2,1,0:T(8,128)}, f32[3,8,128,256]{3,2,1,0:T(8,128)}) fusion(f32[3,8,128,256]{3,2,1,0:T(8,128)} %get-tuple-element.13, f32[3,8,128,256]{3,2,1,0:T(8,128)} %get-tuple-element.7, f32[]{:T(128)S(6)} %div.31, f32[3,8,128,256]{3,2,1,0:T(8,128)} %copy-done.7, f32[3,8,128,256]{3,2,1,0:T(8,128)} %copy-done.6, ...), kind=kLoop, calls=%fused_computation.33 | loop fusion | flops 5505024 | bytes 22020108 | tf_op jit(solution)/shard_map/sub | solution.py:88
  (56 shorter events, 0.4 us)
Async XLA Ops:
  2.0 29.2 %copy-start.2 = (f32[8,128,256]{2,1,0:T(8,128)}, f32[8,128,256]{2,1,0:T(8,128)S(1)}, u32[]{:S(2)}) copy-start(f32[8,128,256]{2,1,0:T(8,128)S(1)} %compare_convert_fusion) | copy-start | bytes 3145732
  4.6 3.0 copy-start.5
  4.6 8.0 %collective-permute-start = (f32[3,1,128,256]{3,2,1,0:T(8,128)S(1)}, f32[3,1,128,256]{3,2,1,0:T(8,128)S(1)}, u32[]{:S(2)}, u32[]{:S(2)}) collective-permute-start(f32[3,1,128,256]{3,2,1,0:T(8,128)S(1)} %slice.319), channel_id=1, source_target_pairs={{8,0},{16,8},{24,16},{9,1},{17,9},{25,17},{10,2},{18,10},{26,18},{... | collective-permute-start | bytes 1179656 | tf_op jit(solution)/shard_map/ppermute | solution.py:15
  6.0 6.7 %collective-permute-start.1 = (f32[3,8,1,256]{3,2,1,0:T(1,128)S(1)}, f32[3,8,1,256]{3,2,1,0:T(1,128)S(1)}, u32[]{:S(2)}, u32[]{:S(2)}) collective-permute-start(f32[3,8,1,256]{3,2,1,0:T(1,128)S(1)} %slice.324), channel_id=1, source_target_pairs={{1,0},{2,1},{3,2},{4,3},{5,4},{6,5},{7,6},{9,8},{10,9},{11,10},{12... | collective-permute-start | bytes 73736 | tf_op jit(solution)/shard_map/ppermute | solution.py:15
  7.6 1.9 copy-start.15
  9.5 3.2 copy-start.1
  9.5 5.0 %slice-start.4 = ((f32[3,8,128,256]{3,2,1,0:T(8,128)}), f32[3,7,128,256]{3,2,1,0:T(8,128)S(1)}, s32[]{:S(2)}) async-start(f32[3,8,128,256]{3,2,1,0:T(8,128)} %copy-done.5), calls=%async_computation.4 | async-start | bytes 5505024 | tf_op jit(solution)/shard_map/slice | solution.py:61
  10.3 8.0 %copy-start = (f32[6,8,128,256]{3,2,1,0:T(8,128)}, f32[6,8,128,256]{3,2,1,0:T(8,128)S(1)}, u32[]{:S(2)}) copy-start(f32[6,8,128,256]{3,2,1,0:T(8,128)S(1)} %convert_element_type.15) | copy-start | bytes 18874372
  10.3 6.2 %copy-start.8 = (bf16[8,128,256]{2,1,0:T(8,128)(2,1)S(1)}, bf16[8,128,256]{2,1,0:T(8,128)(2,1)}, u32[]{:S(2)}) copy-start(bf16[8,128,256]{2,1,0:T(8,128)(2,1)} %param.5) | copy-start | bytes 1572868
  19.8 9.9 %copy-start.14 = (s32[8,128,256]{2,1,0:T(8,128)S(1)}, s32[8,128,256]{2,1,0:T(8,128)}, u32[]{:S(2)}) copy-start(s32[8,128,256]{2,1,0:T(8,128)} %param.7) | copy-start | bytes 3145732
  21.1 10.1 %collective-permute-start.2 = (f32[3,1,128,256]{3,2,1,0:T(8,128)S(1)}, f32[3,1,128,256]{3,2,1,0:T(8,128)S(1)}, u32[]{:S(2)}, u32[]{:S(2)}) collective-permute-start(f32[3,1,128,256]{3,2,1,0:T(8,128)S(1)} %slice.338), channel_id=1, source_target_pairs={{0,8},{8,16},{16,24},{1,9},{9,17},{17,25},{2,10},{10,18},{18,26},{... | collective-permute-start | bytes 1179656 | tf_op jit(solution)/shard_map/ppermute | solution.py:15
  24.2 7.0 %collective-permute-start.3 = (f32[3,8,1,256]{3,2,1,0:T(1,128)S(1)}, f32[3,8,1,256]{3,2,1,0:T(1,128)S(1)}, u32[]{:S(2)}, u32[]{:S(2)}) collective-permute-start(f32[3,8,1,256]{3,2,1,0:T(1,128)S(1)} %slice.340), channel_id=1, source_target_pairs={{0,1},{1,2},{2,3},{3,4},{4,5},{5,6},{6,7},{8,9},{9,10},{10,11},{11... | collective-permute-start | bytes 73736 | tf_op jit(solution)/shard_map/ppermute | solution.py:15
  29.9 5.8 %copy-start.11 = (f32[8,128,256]{2,1,0:T(8,128)}, f32[8,128,256]{2,1,0:T(8,128)S(1)}, u32[]{:S(2)}) copy-start(f32[8,128,256]{2,1,0:T(8,128)S(1)} %select_select_fusion) | copy-start | bytes 3145732
  129.0 24.0 %copy-start.6 = (f32[3,8,128,256]{3,2,1,0:T(8,128)}, f32[3,8,128,256]{3,2,1,0:T(8,128)S(1)}, u32[]{:S(2)}) copy-start(f32[3,8,128,256]{3,2,1,0:T(8,128)S(1)} %get-tuple-element.19) | copy-start | bytes 9437188
  129.0 7.5 %collective-permute-start.4 = (f32[3,1,128,256]{3,2,1,0:T(8,128)S(1)}, f32[3,1,128,256]{3,2,1,0:T(8,128)S(1)}, u32[]{:S(2)}, u32[]{:S(2)}) collective-permute-start(f32[3,1,128,256]{3,2,1,0:T(8,128)S(1)} %slice.344), channel_id=1, source_target_pairs={{8,0},{16,8},{24,16},{9,1},{17,9},{25,17},{10,2},{18,10},{26,18},{... | collective-permute-start | bytes 1179656 | tf_op jit(solution)/shard_map/ppermute | solution.py:15
  130.3 6.2 %collective-permute-start.5 = (f32[3,8,1,256]{3,2,1,0:T(1,128)S(1)}, f32[3,8,1,256]{3,2,1,0:T(1,128)S(1)}, u32[]{:S(2)}, u32[]{:S(2)}) collective-permute-start(f32[3,8,1,256]{3,2,1,0:T(1,128)S(1)} %slice.347), channel_id=1, source_target_pairs={{1,0},{2,1},{3,2},{4,3},{5,4},{6,5},{7,6},{9,8},{10,9},{11,10},{12... | collective-permute-start | bytes 73736 | tf_op jit(solution)/shard_map/ppermute | solution.py:15
  134.4 5.3 %slice-start = ((s8[6291456]{0:T(1024)(128)(4,1)}), s8[4194304]{0:T(1024)(128)(4,1)S(1)}, s32[]{:S(2)}) async-start(s8[6291456]{0:T(1024)(128)(4,1)} %bitcast.270), calls=%async_computation | async-start | bytes 8388608
  134.7 5.0 %slice-start.1 = ((s8[6291456]{0:T(1024)(128)(4,1)}), s8[2097152]{0:T(1024)(128)(4,1)S(1)}, s32[]{:S(2)}) async-start(s8[6291456]{0:T(1024)(128)(4,1)} %bitcast.270), calls=%async_computation.1 | async-start | bytes 4194304
  134.7 5.0 %copy-start.9 = (bf16[8,128,256]{2,1,0:T(8,128)(2,1)S(1)}, bf16[8,128,256]{2,1,0:T(8,128)(2,1)}, u32[]{:S(2)}) copy-start(bf16[8,128,256]{2,1,0:T(8,128)(2,1)} %param.5) | copy-start | bytes 1572868
  143.8 9.2 %copy-start.3 = (f32[8,128,256]{2,1,0:T(8,128)S(1)}, f32[8,128,256]{2,1,0:T(8,128)}, u32[]{:S(2)}) copy-start(f32[8,128,256]{2,1,0:T(8,128)} %copy-done.2) | copy-start | bytes 3145732
  143.8 9.2 %copy-start.12 = (f32[8,128,256]{2,1,0:T(8,128)S(1)}, f32[8,128,256]{2,1,0:T(8,128)}, u32[]{:S(2)}) copy-start(f32[8,128,256]{2,1,0:T(8,128)} %copy-done.11) | copy-start | bytes 3145732
  143.8 9.1 %collective-permute-start.6 = (f32[3,1,128,256]{3,2,1,0:T(8,128)S(1)}, f32[3,1,128,256]{3,2,1,0:T(8,128)S(1)}, u32[]{:S(2)}, u32[]{:S(2)}) collective-permute-start(f32[3,1,128,256]{3,2,1,0:T(8,128)S(1)} %slice.357), channel_id=1, source_target_pairs={{0,8},{8,16},{16,24},{1,9},{9,17},{17,25},{2,10},{10,18},{18,26},{... | collective-permute-start | bytes 1179656 | tf_op jit(solution)/shard_map/ppermute | solution.py:15
  148.1 4.8 %collective-permute-start.7 = (f32[3,8,1,256]{3,2,1,0:T(1,128)S(1)}, f32[3,8,1,256]{3,2,1,0:T(1,128)S(1)}, u32[]{:S(2)}, u32[]{:S(2)}) collective-permute-start(f32[3,8,1,256]{3,2,1,0:T(1,128)S(1)} %slice.359), channel_id=1, source_target_pairs={{0,1},{1,2},{2,3},{3,4},{4,5},{5,6},{6,7},{8,9},{9,10},{10,11},{11... | collective-permute-start | bytes 73736 | tf_op jit(solution)/shard_map/ppermute | solution.py:15
  251.0 23.8 %copy-start.7 = (f32[3,8,128,256]{3,2,1,0:T(8,128)}, f32[3,8,128,256]{3,2,1,0:T(8,128)S(1)}, u32[]{:S(2)}) copy-start(f32[3,8,128,256]{3,2,1,0:T(8,128)S(1)} %get-tuple-element.11) | copy-start | bytes 9437188
  251.1 7.5 %collective-permute-start.8 = (f32[3,1,128,256]{3,2,1,0:T(8,128)S(1)}, f32[3,1,128,256]{3,2,1,0:T(8,128)S(1)}, u32[]{:S(2)}, u32[]{:S(2)}) collective-permute-start(f32[3,1,128,256]{3,2,1,0:T(8,128)S(1)} %slice.363), channel_id=1, source_target_pairs={{8,0},{16,8},{24,16},{9,1},{17,9},{25,17},{10,2},{18,10},{26,18},{... | collective-permute-start | bytes 1179656 | tf_op jit(solution)/shard_map/ppermute | solution.py:15
  252.4 6.2 %collective-permute-start.9 = (f32[3,8,1,256]{3,2,1,0:T(1,128)S(1)}, f32[3,8,1,256]{3,2,1,0:T(1,128)S(1)}, u32[]{:S(2)}, u32[]{:S(2)}) collective-permute-start(f32[3,8,1,256]{3,2,1,0:T(1,128)S(1)} %slice.366), channel_id=1, source_target_pairs={{1,0},{2,1},{3,2},{4,3},{5,4},{6,5},{7,6},{9,8},{10,9},{11,10},{12... | collective-permute-start | bytes 73736 | tf_op jit(solution)/shard_map/ppermute | solution.py:15
  255.1 5.7 %slice-start.2 = ((s8[6291456]{0:T(1024)(128)(4,1)}), s8[4194304]{0:T(1024)(128)(4,1)S(1)}, s32[]{:S(2)}) async-start(s8[6291456]{0:T(1024)(128)(4,1)} %bitcast.272), calls=%async_computation.2 | async-start | bytes 8388608
  255.4 5.4 %slice-start.3 = ((s8[6291456]{0:T(1024)(128)(4,1)}), s8[2097152]{0:T(1024)(128)(4,1)S(1)}, s32[]{:S(2)}) async-start(s8[6291456]{0:T(1024)(128)(4,1)} %bitcast.272), calls=%async_computation.3 | async-start | bytes 4194304
  255.4 5.4 %copy-start.10 = (bf16[8,128,256]{2,1,0:T(8,128)(2,1)S(1)}, bf16[8,128,256]{2,1,0:T(8,128)(2,1)}, u32[]{:S(2)}) copy-start(bf16[8,128,256]{2,1,0:T(8,128)(2,1)} %param.5) | copy-start | bytes 1572868
  265.0 9.8 %copy-start.4 = (f32[8,128,256]{2,1,0:T(8,128)S(1)}, f32[8,128,256]{2,1,0:T(8,128)}, u32[]{:S(2)}) copy-start(f32[8,128,256]{2,1,0:T(8,128)} %copy-done.2) | copy-start | bytes 3145732
  265.0 9.8 %copy-start.13 = (f32[8,128,256]{2,1,0:T(8,128)S(1)}, f32[8,128,256]{2,1,0:T(8,128)}, u32[]{:S(2)}) copy-start(f32[8,128,256]{2,1,0:T(8,128)} %copy-done.11) | copy-start | bytes 3145732
  265.1 9.7 %collective-permute-start.10 = (f32[3,1,128,256]{3,2,1,0:T(8,128)S(1)}, f32[3,1,128,256]{3,2,1,0:T(8,128)S(1)}, u32[]{:S(2)}, u32[]{:S(2)}) collective-permute-start(f32[3,1,128,256]{3,2,1,0:T(8,128)S(1)} %slice.376), channel_id=1, source_target_pairs={{0,8},{8,16},{16,24},{1,9},{9,17},{17,25},{2,10},{10,18},{18,26},{... | collective-permute-start | bytes 1179656 | tf_op jit(solution)/shard_map/ppermute | solution.py:15
  269.4 5.4 %collective-permute-start.11 = (f32[3,8,1,256]{3,2,1,0:T(1,128)S(1)}, f32[3,8,1,256]{3,2,1,0:T(1,128)S(1)}, u32[]{:S(2)}, u32[]{:S(2)}) collective-permute-start(f32[3,8,1,256]{3,2,1,0:T(1,128)S(1)} %slice.378), channel_id=1, source_target_pairs={{0,1},{1,2},{2,3},{3,4},{4,5},{5,6},{6,7},{8,9},{9,10},{10,11},{11... | collective-permute-start | bytes 73736 | tf_op jit(solution)/shard_map/ppermute | solution.py:15
where the time goes:
time: 333 us; the launch traced here: 331 us
  blocking collectives  207 us (62%)
  other arithmetic  63.6 us (19%)
  starting transfers between devices  32.5 us (10%)
  waiting for transfers between devices  11 us (3%)
  local copies, waits for them, and re-layouts  9.33 us (3%)
  between operations  7.68 us (2%)
    psum x3, blocking collectives, squares(): return lax.psum(jnp.sum(vector * vector), ('gx', 'yz'))  124 us
    psum x2, blocking collectives, per_device(): alpha = norm_now / lax.psum(jnp.sum(direction * image), ('gx', 'yz'))  83 us
    ppermute x12, starting transfers between devices, from_behind(): return lax.ppermute(x, axis, pairs)  32.5 us
    reduce_sum x3, other arithmetic, per_device(): alpha = norm_now / lax.psum(jnp.sum(direction * image), ('gx', 'yz'))  13.1 us
    ppermute x12, waiting for transfers between devices, from_behind(): return lax.ppermute(x, axis, pairs)  11 us
    sub x1, other arithmetic, per_device(): residual = residual - alpha * image  9.53 us
    reduce_sum x2, other arithmetic, squares(): return lax.psum(jnp.sum(vector * vector), ('gx', 'yz'))  9.37 us
    mul x3, other arithmetic, operate_shifts(): masked = mask * field  9.22 us
  transfers between devices with their start and end apart: 12, of which 6 were waited for; matrix products, arithmetic and copies ran while one was open for 2% of the time, Pallas kernels for 0%

commit v1 on v0

v1 whole, which is shorter than its diff:
```python
import functools

import jax
import jax.numpy as jnp
from jax import lax
from jax.experimental import pallas as pl
from jax.experimental.pallas import tpu as pltpu
from jax.sharding import PartitionSpec as P

SOFTEN = 0.8
ROWS = 8
PACKED = 16
RING = 4
UNROLL = 2
MESH = pl.DeviceIdType.MESH

UP_X, DOWN_X, UP_DIAG, DOWN_DIAG, UP_Y, DOWN_Y = 0, 1, 2, 3, 4, 7
MESSAGES = 10
LOW, MID, HIGH = 0, 1, 2


def softening(strain, eta):
    self_dot = (
        strain[0] * strain[0] + strain[1] * strain[1] + strain[2] * strain[2]
        + 2.0 * (strain[3] * strain[3] + strain[4] * strain[4] + strain[5] * strain[5])
    )
    return (2.0 * SOFTEN) * eta / (1.0 + self_dot)


def stress(base, next_x, next_y, next_z, strain, eta, soft):
    along_x = [next_x[c] - base[c] for c in range(3)]
    along_y = [next_y[c] - base[c] for c in range(3)]
    along_z = [next_z[c] - base[c] for c in range(3)]
    parts = [
        along_x[0], along_y[1], along_z[2],
        along_y[0] + along_x[1], along_z[0] + along_x[2], along_z[1] + along_y[2],
    ]
    cross = (
        (strain[0] * parts[0] + strain[1] * parts[1])
        + (strain[2] * parts[2] + strain[3] * parts[3])
        + (strain[4] * parts[4] + strain[5] * parts[5])
    )
    factor = soft * cross
    twice = eta + eta
    return [(twice if k < 3 else eta) * parts[k] - factor * strain[k] for k in range(6)]


def kernel(
    gx_size, yz_size,
    load, viscosity, strain_rate, code,
    field, resid,
    m0, m1, m2, strain, eta, soft, weight, flux,
    raw_s, raw_v, raw_c, edge_xs, edge_xv, edge_ys, edge_yv,
    sums_x, sums_y,
    load_sem, raw_sem, send_sem, recv_sem, edge_send, edge_recv,
    sum_send_x, sum_recv_x, sum_send_y, sum_recv_y,
):
    _, X, Y, Z = load.shape
    blocks = Y // ROWS
    gx = lax.axis_index("gx")
    yz = lax.axis_index("yz")
    low_x, high_x = gx == 0, gx == gx_size - 1
    low_y, high_y = yz == 0, yz == yz_size - 1
    not_ = jnp.logical_not
    both = jnp.logical_and
    above_x, below_x = lax.rem(gx + 1, gx_size), lax.rem(gx + gx_size - 1, gx_size)
    above_y, below_y = lax.rem(yz + 1, yz_size), lax.rem(yz + yz_size - 1, yz_size)
    ring = min(RING, X)

    def layer_of(i):
        return lax.rem(i + X - 1, X)

    def load_copy(x):
        return pltpu.make_async_copy(load.at[:, x], field.at[:, x], load_sem.at[x])

    def raw_copies(i):
        x, slot = layer_of(i), lax.rem(i, ring)
        return (
            pltpu.make_async_copy(strain_rate.at[:, x], raw_s.at[slot], raw_sem.at[0, slot]),
            pltpu.make_async_copy(viscosity.at[x], raw_v.at[slot], raw_sem.at[1, slot]),
            pltpu.make_async_copy(code.at[x], raw_c.at[slot], raw_sem.at[2, slot]),
        )

    for i in range(ring):
        for copy in raw_copies(jnp.int32(i)):
            copy.start()
        load_copy(layer_of(jnp.int32(i))).start()
    for i in range(ring, X):
        load_copy(layer_of(jnp.int32(i))).start()

    barrier = pltpu.get_barrier_semaphore()
    for k in range(1, gx_size):
        pl.semaphore_signal(barrier, inc=1, device_id=(lax.rem(gx + k, gx_size), yz), device_id_type=MESH)
    for k in range(1, yz_size):
        pl.semaphore_signal(barrier, inc=1, device_id=(gx, lax.rem(yz + k, yz_size)), device_id_type=MESH)
    has_up_diag = both(not_(high_x), not_(low_y))
    has_down_diag = both(not_(low_x), not_(high_y))

    for peer in ((above_x, below_y), (below_x, above_y)):
        pl.semaphore_signal(barrier, inc=1, device_id=peer, device_id_type=MESH)

    fields = (m0, m1, m2)

    @pl.when(low_x)
    def _():
        strain[:, 0, ROWS:] = jnp.zeros((6, Y, Z), jnp.float32)
        eta[0, ROWS:] = jnp.zeros((Y, Z), jnp.float32)
        soft[0, ROWS:] = jnp.zeros((Y, Z), jnp.float32)
        for m in fields:
            m[:, 0, ROWS:] = jnp.zeros((3, Y + ROWS, Z), jnp.float32)

    @pl.when(high_x)
    def _():
        for m in fields:
            m[:, X + 1] = jnp.zeros((3, Y + 2 * ROWS, Z), jnp.float32)

    @pl.when(low_y)
    def _():
        strain[:, 1:, :ROWS] = jnp.zeros((6, X, ROWS, Z), jnp.float32)
        eta[1:, :ROWS] = jnp.zeros((X, ROWS, Z), jnp.float32)
        soft[1:, :ROWS] = jnp.zeros((X, ROWS, Z), jnp.float32)
        for m in fields:
            m[:, 1:, :ROWS] = jnp.zeros((3, X + 1, ROWS, Z), jnp.float32)

    @pl.when(high_y)
    def _():
        for m in fields:
            m[:, :X + 1, Y + ROWS:] = jnp.zeros((3, X + 1, ROWS, Z), jnp.float32)

    pl.semaphore_wait(barrier, gx_size - 1 + yz_size - 1 + 2)

    def edge(i):
        src, dst, to = (
            (strain_rate.at[:, X - 1], edge_xs, (above_x, yz)),
            (viscosity.at[X - 1], edge_xv, (above_x, yz)),
            (strain_rate.at[:, :, pl.ds(Y - PACKED, PACKED)], edge_ys, (gx, above_y)),
            (viscosity.at[:, pl.ds(Y - PACKED, PACKED)], edge_yv, (gx, above_y)),
        )[i]
        return pltpu.make_async_remote_copy(
            src_ref=src, dst_ref=dst, send_sem=edge_send.at[i], recv_sem=edge_recv.at[i],
            device_id=to, device_id_type=MESH,
        )

    @pl.when(not_(high_y))
    def _():
        edge(2).start()
        edge(3).start()

    sends = [not_(high_x), not_(low_x), has_up_diag, has_down_diag] + [not_(high_y)] * 3 + [not_(low_y)] * 3
    recvs = [not_(low_x), not_(high_x), has_down_diag, has_up_diag] + [not_(low_y)] * 3 + [not_(high_y)] * 3

    def message(step, i):
        m = fields[step]
        own = pl.ds(ROWS, Y)
        first, last = pl.ds(ROWS, ROWS), pl.ds(Y, ROWS)
        under, over = pl.ds(0, ROWS), pl.ds(Y + ROWS, ROWS)
        part = (pl.ds(1, 1), pl.ds(2, X - 2), pl.ds(X, 1))
        if i == UP_X:
            src, dst, to = m.at[:, X, own], m.at[:, 0, own], (above_x, yz)
        elif i == DOWN_X:
            src, dst, to = m.at[:, 1, own], m.at[:, X + 1, own], (below_x, yz)
        elif i == UP_DIAG:
            src, dst, to = m.at[:, X, first], m.at[:, 0, over], (above_x, below_y)
        elif i == DOWN_DIAG:
            src, dst, to = m.at[:, 1, last], m.at[:, X + 1, under], (below_x, above_y)
        elif i < DOWN_Y:
            src, dst, to = m.at[:, part[i - UP_Y], last], m.at[:, part[i - UP_Y], under], (gx, above_y)
        else:
            src, dst, to = m.at[:, part[i - DOWN_Y], first], m.at[:, part[i - DOWN_Y], over], (gx, below_y)
        return pltpu.make_async_remote_copy(
            src_ref=src, dst_ref=dst, send_sem=send_sem.at[step, i], recv_sem=recv_sem.at[step, i],
            device_id=to, device_id_type=MESH,
        )

    def send(step, which):
        for i in which:
            @pl.when(sends[i])
            def _(i=i):
                message(step, i).start()

    def receive(step, which):
        for i in which:
            @pl.when(recvs[i])
            def _(i=i):
                message(step, i).wait_recv()

    to_high = (UP_X, UP_DIAG, UP_Y + HIGH, DOWN_Y + HIGH)
    to_low = (DOWN_X, DOWN_DIAG, UP_Y + LOW, DOWN_Y + LOW)
    to_mid = (UP_Y + MID, DOWN_Y + MID)

    zero = jnp.zeros((ROWS, Z), jnp.float32)

    def prepare(i, sums):
        x, slot = layer_of(i), lax.rem(i, ring)
        for copy in raw_copies(i):
            copy.wait()
        load_copy(x).wait()

        def body(j, sums):
            held, free = sums
            here = pl.ds(pl.multiple_of(j * PACKED, PACKED), PACKED)
            there = pl.ds(pl.multiple_of(j * PACKED + ROWS, ROWS), PACKED)
            s = [raw_s[slot, k, here].astype(jnp.float32) for k in range(6)]
            v = raw_v[slot, here].astype(jnp.float32)
            kind = raw_c[slot, here]
            pin = kind == 0
            for k in range(6):
                strain[k, x + 1, there] = s[k]
            eta[x + 1, there] = v
            soft[x + 1, there] = softening(s, v)
            weight[x, here] = jnp.where(pin, 0.0, jnp.where(kind == 1, 0.2, 1.2)).astype(jnp.float32)
            for c in range(3):
                b = field[c, x, here]
                m = jnp.where(pin, 0.0, b)
                p = jnp.where(pin, b, 0.0)
                m0[c, x + 1, there] = m
                m, p = m * m, p * p
                free = free + (m[:ROWS] + m[ROWS:])
                held = held + (p[:ROWS] + p[ROWS:])
            return held, free

        sums = lax.fori_loop(0, Y // PACKED, body, sums)

        @pl.when(i + ring < X)
        def _():
            for copy in raw_copies(i + ring):
                copy.start()

        return sums

    sums = prepare(jnp.int32(0), (zero, zero))
    send(0, to_high)

    @pl.when(not_(high_x))
    def _():
        edge(0).start()
        edge(1).start()

    sums = prepare(jnp.int32(1), sums)
    send(0, to_low)
    held, free = lax.fori_loop(2, X, prepare, sums)
    send(0, to_mid)

    row = lax.broadcasted_iota(jnp.int32, (ROWS, Z), 0)
    lane = lax.broadcasted_iota(jnp.int32, (ROWS, Z), 1)
    top_row, bottom_row = row == 0, row == ROWS - 1
    first_lane, last_lane = lane == 0, lane == Z - 1

    def rows(j):
        return pl.ds(pl.multiple_of(j * ROWS, ROWS), ROWS)

    def tau(m, x, j, base, up):
        here = rows(j)
        next_x = [m[c, x + 1, here] for c in range(3)]
        next_y = [pltpu.roll(jnp.where(top_row, up[c], base[c]), ROWS - 1, 0) for c in range(3)]
        next_z = [jnp.where(last_lane, 0.0, pltpu.roll(base[c], Z - 1, 1)) for c in range(3)]
        s = [strain[k, x, here] for k in range(6)]
        return stress(base, next_x, next_y, next_z, s, eta[x, here], soft[x, here])

    def block(m, x, j):
        return tuple(m[c, x, rows(j)] for c in range(3))

    def flux_layer(m, x):
        def body(j, base):
            up = block(m, x, j + 1)
            t = tau(m, x, j, base, up)
            for c, k in enumerate((0, 3, 4)):
                flux[c, rows(j - 1)] = t[k]
            return up

        lax.fori_loop(1, blocks + 1, body, block(m, x, 1))

    def image_layer(m, out, shift, x, sums):
        base = block(m, x, 0)
        up = block(m, x, 1)
        t = tau(m, x, 0, base, up)

        def body(j, carry):
            base, prev, one, two = carry
            up = block(m, x, j + 1)
            t = tau(m, x, j, base, up)
            fx, fy, fz = (t[0], t[3], t[4]), (t[3], t[1], t[5]), (t[4], t[5], t[2])
            w = weight[x - 1, rows(j - 1)]
            kept = w > 0.0
            for c in range(3):
                before_x = flux[c, rows(j - 1)]
                before_y = pltpu.roll(jnp.where(bottom_row, prev[c], fy[c]), 1, 0)
                before_z = jnp.where(first_lane, 0.0, pltpu.roll(fz[c], 1, 1))
                value = (before_x - fx[c]) + (before_y - fy[c]) + (before_z - fz[c]) + w * base[c]
                value = jnp.where(kept, value, 0.0)
                flux[c, rows(j - 1)] = fx[c]
                out[c, x - shift, rows(j - shift)] = value
                one = one + base[c] * value
                two = two + value * value
            return up, fy, one, two

        carry = (up, (t[3], t[1], t[5])) + sums
        return lax.fori_loop(1, blocks + 1, body, carry, unroll=UNROLL)[2:]

    def edge_block(raw, shown, dst):
        s, v = raw
        s = [a.astype(jnp.float32)[shown] for a in s]
        v = v.astype(jnp.float32)[shown]
        x, at = dst
        for k in range(6):
            strain[k, x, at] = s[k]
        eta[x, at] = v
        soft[x, at] = softening(s, v)

    totals = [held, free]
    for step in range(3):
        m = fields[step]
        out, shift = (fields[step + 1], 0) if step < 2 else (resid, 1)
        receive(step, to_mid + (UP_Y + LOW, DOWN_Y + LOW, UP_Y + HIGH, DOWN_Y + HIGH))
        if step == 0:
            @pl.when(not_(low_y))
            def _():
                edge(2).wait_recv()
                edge(3).wait_recv()

                @pl.loop(0, X)
                def _(x):
                    raw = [edge_ys[k, x] for k in range(6)], edge_yv[x]
                    edge_block(raw, slice(PACKED - ROWS, PACKED), (x + 1, pl.ds(0, ROWS)))

        sums = (zero, zero)
        flux_layer(m, 1)
        sums = lax.fori_loop(2, X, functools.partial(image_layer, m, out, shift), sums)
        if step < 2:
            send(step + 1, to_mid)
        receive(step, (DOWN_X, DOWN_DIAG))
        sums = image_layer(m, out, shift, X, sums)
        if step < 2:
            send(step + 1, to_high)
        receive(step, (UP_X, UP_DIAG))
        if step == 0:
            @pl.when(not_(low_x))
            def _():
                edge(0).wait_recv()
                edge(1).wait_recv()

                @pl.loop(0, Y // PACKED)
                def _(j):
                    at = pl.ds(pl.multiple_of(j * PACKED, PACKED), PACKED)
                    raw = [edge_xs[k, at] for k in range(6)], edge_xv[at]
                    to = pl.ds(pl.multiple_of(j * PACKED + ROWS, ROWS), PACKED)
                    edge_block(raw, slice(0, PACKED), (0, to))

        flux_layer(m, 0)
        sums = image_layer(m, out, shift, 1, sums)
        if step < 2:
            send(step + 1, to_low)
        totals += list(sums)

    totals = totals[:7]
    lines = [sum(jnp.sum(a, 0, keepdims=True)[:, k:k + 128] for k in range(0, Z, 128)) for a in totals]
    number = lax.broadcasted_iota(jnp.int32, (8, 128), 0)
    tile = jnp.zeros((8, 128), jnp.float32)
    for k, line in enumerate(lines):
        tile = jnp.where(number == k, jnp.broadcast_to(line, (8, 128)), tile)

    def exchange(buf, axis, me, size, send_s, recv_s, tile):
        buf[me] = tile

        def copy(k):
            peer = lax.rem(me + k, size)
            to = (peer, yz) if axis == 0 else (gx, peer)
            return pltpu.make_async_remote_copy(
                src_ref=buf.at[me], dst_ref=buf.at[me], send_sem=send_s.at[k - 1],
                recv_sem=recv_s.at[k - 1], device_id=to, device_id_type=MESH,
            )

        def arrival(k):
            peer = lax.rem(me + size - k, size)
            to = (peer, yz) if axis == 0 else (gx, peer)
            return pltpu.make_async_remote_copy(
                src_ref=buf.at[peer], dst_ref=buf.at[peer], send_sem=send_s.at[k - 1],
                recv_sem=recv_s.at[k - 1], device_id=to, device_id_type=MESH,
            )

        for k in range(1, size):
            copy(k).start()
        for k in range(1, size):
            arrival(k).wait_recv()
        total = buf[0]
        for k in range(1, size):
            total = total + buf[k]
        for k in range(1, size):
            copy(k).wait_send()
        return total

    tile = exchange(sums_x, 0, gx, gx_size, sum_send_x, sum_recv_x, tile)
    tile = exchange(sums_y, 1, yz, yz_size, sum_send_y, sum_recv_y, tile)
    tile = jnp.sum(tile, axis=1, keepdims=True)
    pinned = tile[0:1]
    mu = [tile[k:k + 1] + pinned for k in range(1, 7)]

    scale = mu[1] / mu[0]
    n, power = [], jnp.ones_like(scale)
    for k in range(6):
        n.append(mu[k] / mu[0] / power)
        power = power * scale
    a11, a12, a22 = n[3] - n[2] * n[2], n[4] - n[2] * n[3], n[5] - n[3] * n[3]
    y1, y2 = 1.0 - n[2], n[2] - n[3]
    ratio = a12 / a11
    c2 = (y2 - ratio * y1) / (a22 - ratio * a12)
    c1 = (y1 - a12 * c2) / a11
    c0 = 1.0 - n[2] * c1 - n[3] * c2
    c0, c1, c2 = [
        jnp.broadcast_to(c, (ROWS, Z))
        for c in (c0 / scale, c1 / scale / scale, c2 / scale / scale / scale)
    ]

    @pl.loop(0, X)
    def _(x):
        @pl.loop(0, blocks)
        def _(j):
            here, there = rows(j), rows(j + 1)
            kept = weight[x, here] > 0.0
            for c in range(3):
                v0 = field[c, x, here]
                v1 = jnp.where(kept, m1[c, x + 1, there], v0)
                v2 = jnp.where(kept, m2[c, x + 1, there], v0)
                v3 = jnp.where(kept, resid[c, x, here], v0)
                field[c, x, here] = c0 * v0 + c1 * v1 + c2 * v2
                resid[c, x, here] = v0 - c0 * v1 - c1 * v2 - c2 * v3

    for step in range(3):
        for i in range(MESSAGES):
            @pl.when(sends[i])
            def _(step=step, i=i):
                message(step, i).wait_send()

    @pl.when(not_(high_x))
    def _():
        edge(0).wait_send()
        edge(1).wait_send()

    @pl.when(not_(high_y))
    def _():
        edge(2).wait_send()
        edge(3).wait_send()


def solution(mesh):
    gx_size, yz_size = mesh.shape["gx"], mesh.shape["yz"]

    def per_device(right_side, viscosity, strain_rate, cell_code):
        _, X, Y, Z = right_side.shape
        ring = min(RING, X)
        f32, bf16 = jnp.float32, jnp.bfloat16
        result = jax.ShapeDtypeStruct(right_side.shape, f32)
        padded = pltpu.VMEM((3, X + 2, Y + 2 * ROWS, Z), f32)
        dma = pltpu.SemaphoreType.DMA
        return pl.pallas_call(
            functools.partial(kernel, gx_size, yz_size),
            out_shape=(result, result),
            in_specs=[pl.BlockSpec(memory_space=pl.ANY)] * 4,
            out_specs=(pl.BlockSpec(memory_space=pltpu.VMEM),) * 2,
            scratch_shapes=[
                padded, padded, padded,
                pltpu.VMEM((6, X + 1, Y + ROWS, Z), f32),
                pltpu.VMEM((X + 1, Y + ROWS, Z), f32),
                pltpu.VMEM((X + 1, Y + ROWS, Z), f32),
                pltpu.VMEM((X, Y, Z), f32),
                pltpu.VMEM((3, Y, Z), f32),
                pltpu.VMEM((ring, 6, Y, Z), bf16),
                pltpu.VMEM((ring, Y, Z), bf16),
                pltpu.VMEM((ring, Y, Z), jnp.int32),
                pltpu.VMEM((6, Y, Z), bf16),
                pltpu.VMEM((Y, Z), bf16),
                pltpu.VMEM((6, X, PACKED, Z), bf16),
                pltpu.VMEM((X, PACKED, Z), bf16),
                pltpu.VMEM((gx_size, 8, 128), f32),
                pltpu.VMEM((yz_size, 8, 128), f32),
                dma((X,)), dma((3, ring)),
                dma((3, MESSAGES)), dma((3, MESSAGES)),
                dma((4,)), dma((4,)),
                dma((gx_size - 1,)), dma((gx_size - 1,)),
                dma((yz_size - 1,)), dma((yz_size - 1,)),
            ],
            compiler_params=pltpu.CompilerParams(
                collective_id=0, has_side_effects=True, vmem_limit_bytes=63 * 1024 * 1024,
            ),
        )(right_side, viscosity, strain_rate, cell_code)

    placed = (
        P(None, "gx", "yz", None),
        P("gx", "yz", None),
        P(None, "gx", "yz", None),
        P("gx", "yz", None),
    )
    return jax.shard_map(
        per_device,
        mesh=mesh,
        in_specs=placed,
        out_specs=(P(None, "gx", "yz", None), P(None, "gx", "yz", None)),
        check_vma=False,
    )
```

time: 333 us -> 102 us (0.31)
  blocking collectives: 207 us -> 0 us
  Pallas kernels: 0 us -> 95.8 us
  other arithmetic: 63.6 us -> 0 us
  starting transfers between devices: 32.5 us -> 0 us
  waiting for transfers between devices: 11 us -> 0 us
  between operations: 7.68 us -> 0.65 us
  local copies, waits for them, and re-layouts: 9.33 us -> 5.68 us
    psum x5 -> x0, blocking collectives: 207 us -> none  [the longest x3 124 us: squares(): return lax.psum(jnp.sum(vector * vector), ('gx', 'yz'))]
    pallas_call x0 -> x1, Pallas kernels: none -> 95.8 us  [per_device(): pl.pallas_call(functools.partial(kernel, gx_size, yz_size), out_shape=(re...]
    ppermute x12 -> x0, starting transfers between devices: 32.5 us -> none  [from_behind(): return lax.ppermute(x, axis, pairs)]
    reduce_sum x5 -> x0, other arithmetic: 22.5 us -> none  [the longest x3 13.1 us: per_device(): alpha = norm_now / lax.psum(jnp.sum(direction * image), ('gx', 'yz'))]
    sub x4 -> x0, other arithmetic: 16.9 us -> none  [the longest x1 9.53 us: per_device(): residual = residual - alpha * image]
    another operation x9 -> x0, other arithmetic: 12.7 us -> none  [the longest x6 7.52 us: stresses(): flux_x = jnp.stack([taus[0], taus[3], taus[4]])]
    ppermute x12 -> x0, waiting for transfers between devices: 11 us -> none  [from_behind(): return lax.ppermute(x, axis, pairs)]
    mul x3 -> x0, other arithmetic: 9.22 us -> none  [operate_shifts(): masked = mask * field]
  transfers between devices with their start and end apart: 12 -> 0, of which waited for: 6 -> 0; matrix products, arithmetic and copies ran while one was open for 2% -> 0% of each run, Pallas kernels for 0% -> 0%
where the time goes in v1:
time: 102 us
  Pallas kernels  95.8 us (94%)
  local copies, waits for them, and re-layouts  5.68 us (6%)
    pallas_call x1, Pallas kernels, per_device(): pl.pallas_call(functools.partial(kernel, gx_size, yz_size), out_shape=(re...  95.8 us
    unnamed x4, local copies, waits for them, and re-layouts  5.68 us

profile of v1, /device:TPU:0, one launch (start us, length us, event | category | flops | bytes accessed | tf_op | source)
XLA Modules:
  0.0 102.1 jit_solution(1373166458106059984)
XLA Ops:
  0.6 95.8 %shard_map.59 = (f32[3,8,128,256]{3,2,1,0:T(8,128)}, f32[3,8,128,256]{3,2,1,0:T(8,128)}) custom-call(f32[3,8,128,256]{3,2,1,0:T(8,128)} %load.1, bf16[8,128,256]{2,1,0:T(8,128)(2,1)} %viscosity.1, bf16[6,8,128,256]{3,2,1,0:T(8,128)(2,1)} %strain_rate.1, s32[8,128,256]{2,1,0:T(8,128)} %code.1), custom_call_target="tpu_custom_call" | custom-call | tf_op jit(solution)/shard_map/pallas_call | solution.py:455
  96.4 0.0 copy-start
  96.4 4.0 %copy.8 = f32[3,8,128,256]{3,2,1,0:T(8,128)} copy(f32[3,8,128,256]{3,2,1,0:T(8,128)} %get-tuple-element.4) | data formatting | bytes 6291456
  100.5 0.0 copy-done
  100.5 1.7 %copy.9 = f32[3,8,128,256]{3,2,1,0:T(8,128)} copy(f32[3,8,128,256]{3,2,1,0:T(8,128)S(1)} %copy-done) | data formatting | bytes 6291456
Async XLA Ops:
  96.4 4.0 %copy-start = (f32[3,8,128,256]{3,2,1,0:T(8,128)S(1)}, f32[3,8,128,256]{3,2,1,0:T(8,128)}, u32[]{:S(2)}) copy-start(f32[3,8,128,256]{3,2,1,0:T(8,128)} %get-tuple-element.5) | copy-start | bytes 9437188

commit v2 on v1

--- a/solution.py
+++ b/solution.py
@@ -11,7 +11,7 @@
 ROWS = 8
 PACKED = 16
 RING = 4
-UNROLL = 2
+UNROLL = 4
 MESH = pl.DeviceIdType.MESH
 
 UP_X, DOWN_X, UP_DIAG, DOWN_DIAG, UP_Y, DOWN_Y = 0, 1, 2, 3, 4, 7
@@ -219,7 +219,7 @@
                 held = held + (p[:ROWS] + p[ROWS:])
             return held, free
 
-        sums = lax.fori_loop(0, Y // PACKED, body, sums)
+        sums = lax.fori_loop(0, Y // PACKED, body, sums, unroll=UNROLL)
 
         @pl.when(i + ring < X)
         def _():
@@ -247,7 +247,7 @@
     first_lane, last_lane = lane == 0, lane == Z - 1
 
     def rows(j):
-        return pl.ds(pl.multiple_of(j * ROWS, ROWS), ROWS)
+        return pl.ds(j * ROWS, ROWS)
 
     def tau(m, x, j, base, up):
         here = rows(j)
@@ -261,22 +261,21 @@
         return tuple(m[c, x, rows(j)] for c in range(3))
 
     def flux_layer(m, x):
-        def body(j, base):
+        base = block(m, x, 1)
+        for j in range(1, blocks + 1):
             up = block(m, x, j + 1)
             t = tau(m, x, j, base, up)
             for c, k in enumerate((0, 3, 4)):
                 flux[c, rows(j - 1)] = t[k]
-            return up
-
-        lax.fori_loop(1, blocks + 1, body, block(m, x, 1))
+            base = up
 
     def image_layer(m, out, shift, x, sums):
+        one, two = sums
         base = block(m, x, 0)
         up = block(m, x, 1)
         t = tau(m, x, 0, base, up)
-
-        def body(j, carry):
-            base, prev, one, two = carry
+        base, prev = up, (t[3], t[1], t[5])
+        for j in range(1, blocks + 1):
             up = block(m, x, j + 1)
             t = tau(m, x, j, base, up)
             fx, fy, fz = (t[0], t[3], t[4]), (t[3], t[1], t[5]), (t[4], t[5], t[2])
@@ -292,10 +291,8 @@
                 out[c, x - shift, rows(j - shift)] = value
                 one = one + base[c] * value
                 two = two + value * value
-            return up, fy, one, two
-
-        carry = (up, (t[3], t[1], t[5])) + sums
-        return lax.fori_loop(1, blocks + 1, body, carry, unroll=UNROLL)[2:]
+            base, prev = up, fy
+        return one, two
 
     def edge_block(raw, shown, dst):
         s, v = raw
@@ -306,6 +303,19 @@
             strain[k, x, at] = s[k]
         eta[x, at] = v
         soft[x, at] = softening(s, v)
+
+    def coefficients_below():
+        @pl.when(not_(low_x))
+        def _():
+            edge(0).wait_recv()
+            edge(1).wait_recv()
+
+            @pl.loop(0, Y // PACKED)
+            def _(j):
+                at = pl.ds(pl.multiple_of(j * PACKED, PACKED), PACKED)
+                raw = [edge_xs[k, at] for k in range(6)], edge_xv[at]
+                to = pl.ds(pl.multiple_of(j * PACKED + ROWS, ROWS), PACKED)
+                edge_block(raw, slice(0, PACKED), (0, to))
 
     totals = [held, free]
     for step in range(3):
@@ -323,31 +333,30 @@
                     raw = [edge_ys[k, x] for k in range(6)], edge_yv[x]
                     edge_block(raw, slice(PACKED - ROWS, PACKED), (x + 1, pl.ds(0, ROWS)))
 
-        sums = (zero, zero)
-        flux_layer(m, 1)
-        sums = lax.fori_loop(2, X, functools.partial(image_layer, m, out, shift), sums)
-        if step < 2:
-            send(step + 1, to_mid)
-        receive(step, (DOWN_X, DOWN_DIAG))
-        sums = image_layer(m, out, shift, X, sums)
-        if step < 2:
-            send(step + 1, to_high)
-        receive(step, (UP_X, UP_DIAG))
-        if step == 0:
-            @pl.when(not_(low_x))
+        def turn(t, sums, step=step, m=m, out=out, shift=shift):
+            x = lax.rem(t + 1, X) + 1
+
+            @pl.when(t == X - 2)
             def _():
-                edge(0).wait_recv()
-                edge(1).wait_recv()
-
-                @pl.loop(0, Y // PACKED)
-                def _(j):
-                    at = pl.ds(pl.multiple_of(j * PACKED, PACKED), PACKED)
-                    raw = [edge_xs[k, at] for k in range(6)], edge_xv[at]
-                    to = pl.ds(pl.multiple_of(j * PACKED + ROWS, ROWS), PACKED)
-                    edge_block(raw, slice(0, PACKED), (0, to))
-
-        flux_layer(m, 0)
-        sums = image_layer(m, out, shift, 1, sums)
+                if step < 2:
+                    send(step + 1, to_mid)
+                receive(step, (DOWN_X, DOWN_DIAG))
+
+            @pl.when(t == X - 1)
+            def _():
+                if step < 2:
+                    send(step + 1, to_high)
+                receive(step, (UP_X, UP_DIAG))
+                if step == 0:
+                    coefficients_below()
+
+            @pl.when(jnp.logical_or(t == 0, t == X - 1))
+            def _():
+                flux_layer(m, x - 1)
+
+            return image_layer(m, out, shift, x, sums)
+
+        sums = lax.fori_loop(0, X, turn, (zero, zero))
         if step < 2:
             send(step + 1, to_low)
         totals += list(sums)
@@ -413,8 +422,7 @@
 
     @pl.loop(0, X)
     def _(x):
-        @pl.loop(0, blocks)
-        def _(j):
+        for j in range(blocks):
             here, there = rows(j), rows(j + 1)
             kept = weight[x, here] > 0.0
             for c in range(3):
@@ -449,7 +457,7 @@
         _, X, Y, Z = right_side.shape
         ring = min(RING, X)
         f32, bf16 = jnp.float32, jnp.bfloat16
-        result = jax.ShapeDtypeStruct(right_side.shape, f32)
+        result = pltpu.VMEM(right_side.shape, f32)
         padded = pltpu.VMEM((3, X + 2, Y + 2 * ROWS, Z), f32)
         dma = pltpu.SemaphoreType.DMA
         return pl.pallas_call(
@@ -480,7 +488,7 @@
                 dma((yz_size - 1,)), dma((yz_size - 1,)),
             ],
             compiler_params=pltpu.CompilerParams(
-                collective_id=0, has_side_effects=True, vmem_limit_bytes=63 * 1024 * 1024,
+                collective_id=0, has_side_effects=True, vmem_limit_bytes=50 * 1024 * 1024,
             ),
         )(right_side, viscosity, strain_rate, cell_code)
 

time: 102 us -> 72.9 us (0.71)
  Pallas kernels: 95.8 us -> 68.8 us
  local copies, waits for them, and re-layouts: 5.68 us -> 3.33 us
    pallas_call x1, Pallas kernels: 95.8 us -> 68.8 us  [per_device(): pl.pallas_call(functools.partial(kernel, gx_size, yz_size), out_shape=(re...]
    unnamed x4 -> x2, local copies, waits for them, and re-layouts: 5.68 us -> 3.33 us
where the time goes in v2:
time: 72.9 us; the launch traced here: 72.8 us
  Pallas kernels  68.8 us (94%)
  local copies, waits for them, and re-layouts  3.33 us (5%)
    pallas_call x1, Pallas kernels, per_device(): pl.pallas_call(functools.partial(kernel, gx_size, yz_size), out_shape=(re...  68.8 us
    unnamed x2, local copies, waits for them, and re-layouts  3.33 us

profile of v2, /device:TPU:0, one launch (start us, length us, event | category | flops | bytes accessed | tf_op | source)
XLA Modules:
  0.0 72.8 jit_solution(2109436481397153320)
XLA Ops:
  0.6 68.8 %shard_map.59 = (f32[3,8,128,256]{3,2,1,0:T(8,128)S(1)}, f32[3,8,128,256]{3,2,1,0:T(8,128)S(1)}) custom-call(f32[3,8,128,256]{3,2,1,0:T(8,128)} %load.1, bf16[8,128,256]{2,1,0:T(8,128)(2,1)} %viscosity.1, bf16[6,8,128,256]{3,2,1,0:T(8,128)(2,1)} %strain_rate.1, s32[8,128,256]{2,1,0:T(8,128)} %code.1), custom_call_target="tpu_custom_call" | custom-call | tf_op jit(solution)/shard_map/pallas_call | solution.py:463
  69.4 1.7 %copy.8 = f32[3,8,128,256]{3,2,1,0:T(8,128)} copy(f32[3,8,128,256]{3,2,1,0:T(8,128)S(1)} %get-tuple-element.2) | data formatting | bytes 6291456
  71.1 1.7 %copy.9 = f32[3,8,128,256]{3,2,1,0:T(8,128)} copy(f32[3,8,128,256]{3,2,1,0:T(8,128)S(1)} %get-tuple-element.3) | data formatting | bytes 6291456

commit v3 on v2

--- a/solution.py
+++ b/solution.py
@@ -14,9 +14,8 @@
 UNROLL = 4
 MESH = pl.DeviceIdType.MESH
 
-UP_X, DOWN_X, UP_DIAG, DOWN_DIAG, UP_Y, DOWN_Y = 0, 1, 2, 3, 4, 7
-MESSAGES = 10
-LOW, MID, HIGH = 0, 1, 2
+UP_X, DOWN_X, UP_DIAG, DOWN_DIAG, UP_MID, DOWN_MID, UP_ENDS, DOWN_ENDS = range(8)
+MESSAGES = 8
 
 
 def softening(strain, eta):
@@ -50,7 +49,8 @@
     load, viscosity, strain_rate, code,
     field, resid,
     m0, m1, m2, strain, eta, soft, weight, flux,
-    raw_s, raw_v, raw_c, edge_xs, edge_xv, edge_ys, edge_yv,
+    raw_s, raw_v, raw_c, edge_xs, edge_xv, edge_out, edge_in,
+    mid_out, mid_in, ends_out, ends_in,
     sums_x, sums_y,
     load_sem, raw_sem, send_sem, recv_sem, edge_send, edge_recv,
     sum_send_x, sum_recv_x, sum_send_y, sum_recv_y,
@@ -133,28 +133,21 @@
         src, dst, to = (
             (strain_rate.at[:, X - 1], edge_xs, (above_x, yz)),
             (viscosity.at[X - 1], edge_xv, (above_x, yz)),
-            (strain_rate.at[:, :, pl.ds(Y - PACKED, PACKED)], edge_ys, (gx, above_y)),
-            (viscosity.at[:, pl.ds(Y - PACKED, PACKED)], edge_yv, (gx, above_y)),
+            (edge_out, edge_in, (gx, above_y)),
         )[i]
         return pltpu.make_async_remote_copy(
             src_ref=src, dst_ref=dst, send_sem=edge_send.at[i], recv_sem=edge_recv.at[i],
             device_id=to, device_id_type=MESH,
         )
 
-    @pl.when(not_(high_y))
-    def _():
-        edge(2).start()
-        edge(3).start()
-
-    sends = [not_(high_x), not_(low_x), has_up_diag, has_down_diag] + [not_(high_y)] * 3 + [not_(low_y)] * 3
-    recvs = [not_(low_x), not_(high_x), has_down_diag, has_up_diag] + [not_(low_y)] * 3 + [not_(high_y)] * 3
+    sends = [not_(high_x), not_(low_x), has_up_diag, has_down_diag] + [not_(high_y), not_(low_y)] * 2
+    recvs = [not_(low_x), not_(high_x), has_down_diag, has_up_diag] + [not_(low_y), not_(high_y)] * 2
 
     def message(step, i):
         m = fields[step]
         own = pl.ds(ROWS, Y)
         first, last = pl.ds(ROWS, ROWS), pl.ds(Y, ROWS)
         under, over = pl.ds(0, ROWS), pl.ds(Y + ROWS, ROWS)
-        part = (pl.ds(1, 1), pl.ds(2, X - 2), pl.ds(X, 1))
         if i == UP_X:
             src, dst, to = m.at[:, X, own], m.at[:, 0, own], (above_x, yz)
         elif i == DOWN_X:
@@ -163,10 +156,11 @@
             src, dst, to = m.at[:, X, first], m.at[:, 0, over], (above_x, below_y)
         elif i == DOWN_DIAG:
             src, dst, to = m.at[:, 1, last], m.at[:, X + 1, under], (below_x, above_y)
-        elif i < DOWN_Y:
-            src, dst, to = m.at[:, part[i - UP_Y], last], m.at[:, part[i - UP_Y], under], (gx, above_y)
         else:
-            src, dst, to = m.at[:, part[i - DOWN_Y], first], m.at[:, part[i - DOWN_Y], over], (gx, below_y)
+            way = (i - UP_MID) % 2
+            there, here = (mid_out, mid_in) if i < UP_ENDS else (ends_out, ends_in)
+            src, dst = there.at[step, way], here.at[step, way]
+            to = (gx, below_y if way else above_y)
         return pltpu.make_async_remote_copy(
             src_ref=src, dst_ref=dst, send_sem=send_sem.at[step, i], recv_sem=recv_sem.at[step, i],
             device_id=to, device_id_type=MESH,
@@ -184,9 +178,46 @@
             def _(i=i):
                 message(step, i).wait_recv()
 
-    to_high = (UP_X, UP_DIAG, UP_Y + HIGH, DOWN_Y + HIGH)
-    to_low = (DOWN_X, DOWN_DIAG, UP_Y + LOW, DOWN_Y + LOW)
-    to_mid = (UP_Y + MID, DOWN_Y + MID)
+    to_high = (UP_X, UP_DIAG)
+    to_low = (DOWN_X, DOWN_DIAG, UP_ENDS, DOWN_ENDS)
+    to_mid = (UP_MID, DOWN_MID)
+
+    def stage(step, x):
+        m = fields[step]
+        inner = both(x > 1, x < X)
+        for way, at in enumerate((Y + ROWS - 1, ROWS)):
+            line = [m[c, x, pl.ds(at, 1)] for c in range(3)]
+
+            @pl.when(inner)
+            def _(way=way, line=line):
+                for c in range(3):
+                    mid_out[step, way, c, pl.ds(x - 1, 1)] = line[c]
+
+            @pl.when(x == 1)
+            def _(way=way, line=line):
+                for c in range(3):
+                    ends_out[step, way, pl.ds(c, 1)] = line[c]
+
+            @pl.when(x == X)
+            def _(way=way, line=line):
+                for c in range(3):
+                    ends_out[step, way, pl.ds(3 + c, 1)] = line[c]
+
+    def spread(step):
+        m = fields[step]
+        for way, at in enumerate((0, Y + ROWS)):
+            @pl.when(recvs[UP_MID + way])
+            def _(way=way, at=at):
+                message(step, UP_MID + way).wait_recv()
+                for c in range(3):
+                    for x in range(2, X):
+                        line = mid_in[step, way, c, pl.ds(x - 1, 1)]
+                        m[c, x, pl.ds(at, ROWS)] = jnp.broadcast_to(line, (ROWS, Z))
+                message(step, UP_ENDS + way).wait_recv()
+                for c in range(3):
+                    for k, x in ((0, 1), (3, X)):
+                        line = ends_in[step, way, pl.ds(k + c, 1)]
+                        m[c, x, pl.ds(at, ROWS)] = jnp.broadcast_to(line, (ROWS, Z))
 
     zero = jnp.zeros((ROWS, Z), jnp.float32)
 
@@ -221,6 +252,13 @@
 
         sums = lax.fori_loop(0, Y // PACKED, body, sums, unroll=UNROLL)
 
+        stage(0, x + 1)
+        at = pl.ds(Y + ROWS - 1, 1)
+        for k in range(6):
+            edge_out[k, pl.ds(x, 1)] = strain[k, x + 1, at]
+        edge_out[6, pl.ds(x, 1)] = eta[x + 1, at]
+        edge_out[7, pl.ds(x, 1)] = soft[x + 1, at]
+
         @pl.when(i + ring < X)
         def _():
             for copy in raw_copies(i + ring):
@@ -240,6 +278,10 @@
     send(0, to_low)
     held, free = lax.fori_loop(2, X, prepare, sums)
     send(0, to_mid)
+
+    @pl.when(not_(high_y))
+    def _():
+        edge(2).start()
 
     row = lax.broadcasted_iota(jnp.int32, (ROWS, Z), 0)
     lane = lax.broadcasted_iota(jnp.int32, (ROWS, Z), 1)
@@ -321,17 +363,17 @@
     for step in range(3):
         m = fields[step]
         out, shift = (fields[step + 1], 0) if step < 2 else (resid, 1)
-        receive(step, to_mid + (UP_Y + LOW, DOWN_Y + LOW, UP_Y + HIGH, DOWN_Y + HIGH))
+        spread(step)
         if step == 0:
             @pl.when(not_(low_y))
             def _():
                 edge(2).wait_recv()
-                edge(3).wait_recv()
-
-                @pl.loop(0, X)
-                def _(x):
-                    raw = [edge_ys[k, x] for k in range(6)], edge_yv[x]
-                    edge_block(raw, slice(PACKED - ROWS, PACKED), (x + 1, pl.ds(0, ROWS)))
+                for x in range(X):
+                    line = [jnp.broadcast_to(edge_in[k, pl.ds(x, 1)], (ROWS, Z)) for k in range(8)]
+                    for k in range(6):
+                        strain[k, x + 1, pl.ds(0, ROWS)] = line[k]
+                    eta[x + 1, pl.ds(0, ROWS)] = line[6]
+                    soft[x + 1, pl.ds(0, ROWS)] = line[7]
 
         def turn(t, sums, step=step, m=m, out=out, shift=shift):
             x = lax.rem(t + 1, X) + 1
@@ -354,7 +396,10 @@
             def _():
                 flux_layer(m, x - 1)
 
-            return image_layer(m, out, shift, x, sums)
+            sums = image_layer(m, out, shift, x, sums)
+            if step < 2:
+                stage(step + 1, x)
+            return sums
 
         sums = lax.fori_loop(0, X, turn, (zero, zero))
         if step < 2:
@@ -447,7 +492,6 @@
     @pl.when(not_(high_y))
     def _():
         edge(2).wait_send()
-        edge(3).wait_send()
 
 
 def solution(mesh):
@@ -477,13 +521,14 @@
                 pltpu.VMEM((ring, Y, Z), jnp.int32),
                 pltpu.VMEM((6, Y, Z), bf16),
                 pltpu.VMEM((Y, Z), bf16),
-                pltpu.VMEM((6, X, PACKED, Z), bf16),
-                pltpu.VMEM((X, PACKED, Z), bf16),
+                pltpu.VMEM((8, X, Z), f32), pltpu.VMEM((8, X, Z), f32),
+                pltpu.VMEM((3, 2, 3, X, Z), f32), pltpu.VMEM((3, 2, 3, X, Z), f32),
+                pltpu.VMEM((3, 2, 8, Z), f32), pltpu.VMEM((3, 2, 8, Z), f32),
                 pltpu.VMEM((gx_size, 8, 128), f32),
                 pltpu.VMEM((yz_size, 8, 128), f32),
                 dma((X,)), dma((3, ring)),
                 dma((3, MESSAGES)), dma((3, MESSAGES)),
-                dma((4,)), dma((4,)),
+                dma((3,)), dma((3,)),
                 dma((gx_size - 1,)), dma((gx_size - 1,)),
                 dma((yz_size - 1,)), dma((yz_size - 1,)),
             ],

time: 72.9 us -> 47.8 us (0.66)
  Pallas kernels: 68.8 us -> 43.7 us
    pallas_call x1, Pallas kernels: 68.8 us -> 43.7 us  [per_device(): pl.pallas_call(functools.partial(kernel, gx_size, yz_size), out_shape=(re...]
where the time goes in v3:
time: 47.8 us; the launch traced here: 47.7 us
  Pallas kernels  43.7 us (91%)
  local copies, waits for them, and re-layouts  3.33 us (7%)
  between operations  0.64 us (1%)
    pallas_call x1, Pallas kernels, per_device(): pl.pallas_call(functools.partial(kernel, gx_size, yz_size), out_shape=(re...  43.7 us
    unnamed x2, local copies, waits for them, and re-layouts  3.33 us

profile of v3, /device:TPU:0, one launch (start us, length us, event | category | flops | bytes accessed | tf_op | source)
XLA Modules:
  0.0 47.7 jit_solution(5365813608000879543)
XLA Ops:
  0.6 43.7 %shard_map.59 = (f32[3,8,128,256]{3,2,1,0:T(8,128)S(1)}, f32[3,8,128,256]{3,2,1,0:T(8,128)S(1)}) custom-call(f32[3,8,128,256]{3,2,1,0:T(8,128)} %load.1, bf16[8,128,256]{2,1,0:T(8,128)(2,1)} %viscosity.1, bf16[6,8,128,256]{3,2,1,0:T(8,128)(2,1)} %strain_rate.1, s32[8,128,256]{2,1,0:T(8,128)} %code.1), custom_call_target="tpu_custom_call" | custom-call | tf_op jit(solution)/shard_map/pallas_call | solution.py:507
  44.4 1.7 %copy.8 = f32[3,8,128,256]{3,2,1,0:T(8,128)} copy(f32[3,8,128,256]{3,2,1,0:T(8,128)S(1)} %get-tuple-element.2) | data formatting | bytes 6291456
  46.0 1.7 %copy.9 = f32[3,8,128,256]{3,2,1,0:T(8,128)} copy(f32[3,8,128,256]{3,2,1,0:T(8,128)S(1)} %get-tuple-element.3) | data formatting | bytes 6291456

commit v4 on v3

--- a/solution.py
+++ b/solution.py
@@ -16,6 +16,8 @@
 
 UP_X, DOWN_X, UP_DIAG, DOWN_DIAG, UP_MID, DOWN_MID, UP_ENDS, DOWN_ENDS = range(8)
 MESSAGES = 8
+LATE = (1, 1, 2)
+TURN = (1, 2, 3)
 
 
 def softening(strain, eta):
@@ -127,8 +129,6 @@
         for m in fields:
             m[:, :X + 1, Y + ROWS:] = jnp.zeros((3, X + 1, ROWS, Z), jnp.float32)
 
-    pl.semaphore_wait(barrier, gx_size - 1 + yz_size - 1 + 2)
-
     def edge(i):
         src, dst, to = (
             (strain_rate.at[:, X - 1], edge_xs, (above_x, yz)),
@@ -179,12 +179,13 @@
                 message(step, i).wait_recv()
 
     to_high = (UP_X, UP_DIAG)
-    to_low = (DOWN_X, DOWN_DIAG, UP_ENDS, DOWN_ENDS)
+    to_low = (DOWN_X, DOWN_DIAG)
+    to_ends = (UP_ENDS, DOWN_ENDS)
     to_mid = (UP_MID, DOWN_MID)
 
     def stage(step, x):
         m = fields[step]
-        inner = both(x > 1, x < X)
+        inner = x > LATE[step]
         for way, at in enumerate((Y + ROWS - 1, ROWS)):
             line = [m[c, x, pl.ds(at, 1)] for c in range(3)]
 
@@ -193,30 +194,24 @@
                 for c in range(3):
                     mid_out[step, way, c, pl.ds(x - 1, 1)] = line[c]
 
-            @pl.when(x == 1)
+            @pl.when(not_(inner))
             def _(way=way, line=line):
                 for c in range(3):
-                    ends_out[step, way, pl.ds(c, 1)] = line[c]
-
-            @pl.when(x == X)
-            def _(way=way, line=line):
+                    ends_out[step, way, pl.ds(3 * (x - 1) + c, 1)] = line[c]
+
+    def spread(step, kind):
+        m = fields[step]
+        late = LATE[step]
+        for way, at in enumerate((0, Y + ROWS)):
+            @pl.when(recvs[kind + way])
+            def _(way=way, at=at):
+                message(step, kind + way).wait_recv()
                 for c in range(3):
-                    ends_out[step, way, pl.ds(3 + c, 1)] = line[c]
-
-    def spread(step):
-        m = fields[step]
-        for way, at in enumerate((0, Y + ROWS)):
-            @pl.when(recvs[UP_MID + way])
-            def _(way=way, at=at):
-                message(step, UP_MID + way).wait_recv()
-                for c in range(3):
-                    for x in range(2, X):
-                        line = mid_in[step, way, c, pl.ds(x - 1, 1)]
-                        m[c, x, pl.ds(at, ROWS)] = jnp.broadcast_to(line, (ROWS, Z))
-                message(step, UP_ENDS + way).wait_recv()
-                for c in range(3):
-                    for k, x in ((0, 1), (3, X)):
-                        line = ends_in[step, way, pl.ds(k + c, 1)]
+                    for x in range(late + 1, X + 1) if kind == UP_MID else range(1, late + 1):
+                        if kind == UP_MID:
+                            line = mid_in[step, way, c, pl.ds(x - 1, 1)]
+                        else:
+                            line = ends_in[step, way, pl.ds(3 * (x - 1) + c, 1)]
                         m[c, x, pl.ds(at, ROWS)] = jnp.broadcast_to(line, (ROWS, Z))
 
     zero = jnp.zeros((ROWS, Z), jnp.float32)
@@ -267,6 +262,8 @@
         return sums
 
     sums = prepare(jnp.int32(0), (zero, zero))
+    pl.semaphore_wait(barrier, gx_size - 1 + yz_size - 1 + 2)
+
     send(0, to_high)
 
     @pl.when(not_(high_x))
@@ -275,7 +272,7 @@
         edge(1).start()
 
     sums = prepare(jnp.int32(1), sums)
-    send(0, to_low)
+    send(0, to_low + to_ends)
     held, free = lax.fori_loop(2, X, prepare, sums)
     send(0, to_mid)
 
@@ -363,8 +360,10 @@
     for step in range(3):
         m = fields[step]
         out, shift = (fields[step + 1], 0) if step < 2 else (resid, 1)
-        spread(step)
+        spread(step, UP_MID)
         if step == 0:
+            spread(step, UP_ENDS)
+
             @pl.when(not_(low_y))
             def _():
                 edge(2).wait_recv()
@@ -376,34 +375,40 @@
                     soft[x + 1, pl.ds(0, ROWS)] = line[7]
 
         def turn(t, sums, step=step, m=m, out=out, shift=shift):
-            x = lax.rem(t + 1, X) + 1
-
-            @pl.when(t == X - 2)
+            begin = TURN[step]
+            x = lax.rem(t + begin, X) + 1
+
+            @pl.when(t == X - begin - 1)
+            def _():
+                receive(step, (DOWN_X, DOWN_DIAG))
+
+            @pl.when(t == X - begin)
             def _():
                 if step < 2:
-                    send(step + 1, to_mid)
-                receive(step, (DOWN_X, DOWN_DIAG))
-
-            @pl.when(t == X - 1)
-            def _():
-                if step < 2:
-                    send(step + 1, to_high)
+                    send(step + 1, to_high + to_mid)
                 receive(step, (UP_X, UP_DIAG))
                 if step == 0:
                     coefficients_below()
-
-            @pl.when(jnp.logical_or(t == 0, t == X - 1))
+                else:
+                    spread(step, UP_ENDS)
+
+            @pl.when(jnp.logical_or(t == 0, t == X - begin))
             def _():
                 flux_layer(m, x - 1)
 
             sums = image_layer(m, out, shift, x, sums)
             if step < 2:
                 stage(step + 1, x)
+
+                @pl.when(t == X - begin)
+                def _():
+                    send(step + 1, to_low)
+
             return sums
 
         sums = lax.fori_loop(0, X, turn, (zero, zero))
         if step < 2:
-            send(step + 1, to_low)
+            send(step + 1, to_ends)
         totals += list(sums)
 
     totals = totals[:7]

time: 47.8 us -> 47.4 us (level)
  no operation moved by 1% of the time
where the time goes in v4:
time: 47.4 us; the launch traced here: 47.3 us
  Pallas kernels  43.3 us (91%)
  local copies, waits for them, and re-layouts  3.33 us (7%)
  between operations  0.64 us (1%)
    pallas_call x1, Pallas kernels, per_device(): pl.pallas_call(functools.partial(kernel, gx_size, yz_size), out_shape=(re...  43.3 us
    unnamed x2, local copies, waits for them, and re-layouts  3.33 us

profile of v4, /device:TPU:0, one launch (start us, length us, event | category | flops | bytes accessed | tf_op | source)
XLA Modules:
  0.0 47.3 jit_solution(4209514052274637018)
XLA Ops:
  0.6 43.3 %shard_map.59 = (f32[3,8,128,256]{3,2,1,0:T(8,128)S(1)}, f32[3,8,128,256]{3,2,1,0:T(8,128)S(1)}) custom-call(f32[3,8,128,256]{3,2,1,0:T(8,128)} %load.1, bf16[8,128,256]{2,1,0:T(8,128)(2,1)} %viscosity.1, bf16[6,8,128,256]{3,2,1,0:T(8,128)(2,1)} %strain_rate.1, s32[8,128,256]{2,1,0:T(8,128)} %code.1), custom_call_target="tpu_custom_call" | custom-call | tf_op jit(solution)/shard_map/pallas_call | solution.py:512
  44.0 1.7 %copy.8 = f32[3,8,128,256]{3,2,1,0:T(8,128)} copy(f32[3,8,128,256]{3,2,1,0:T(8,128)S(1)} %get-tuple-element.2) | data formatting | bytes 6291456
  45.6 1.7 %copy.9 = f32[3,8,128,256]{3,2,1,0:T(8,128)} copy(f32[3,8,128,256]{3,2,1,0:T(8,128)S(1)} %get-tuple-element.3) | data formatting | bytes 6291456
